TPU v7x, 32 devices: a whole 2x2x4 slice. The times are simulated.
32 devices in a mesh: dp: 8 (over z, x), mp: 4 (over y, core).
Axes of the slice: x: 2, y: 2, z: 4, core: 2. Of those that a mesh axis runs over, the one named last changes fastest.
Arguments:
- query: bfloat16 [2048, 4096], P('dp', 'mp'), may hold values from -400 to 400
- keys_values: bfloat16 [2, 2048, 512], P(None, 'dp'), may hold values from -6 to 6
- ancestors: int32 [16, 12], P('dp'), may hold values from -1 to 15, as said below
- tile_of_slot: int32 [16], replicated, may hold values from 0 to 15, as said below
- residual: bfloat16 [2048, 8192], P('dp', 'mp'), may hold values from -6 to 6
- norm_gain: float32 [8192], P('mp'), may hold values from 0.25 to 1.75
- out_weight: bfloat16 [4096, 8192], P('mp'), may hold values from -0.09375 to 0.09375
Outputs:
- hidden_out: bfloat16 [2048, 8192], P('dp', 'mp')
- normed: bfloat16 [2048, 8192], P('dp', 'mp')
Inputs may be any that keep to these rules, and one draw needn't show every extreme that they name: Ids of tiles, or -1. Over all query tiles of one device's 2 positions, the ancestors that lie at the positions of any one device number at most 1 distinct tiles; some device reaches 1 in every draw. `tile_of_slot`: a permutation of the tile ids.
All inputs are finite; a program needn't handle non-finite values.
Results may differ from a plain program's by a relative error of at most 0.008.
Values may be sent and summed in bfloat16 or wider, within the bound.
A program may use at most 64 MiB of HBM per device.

v0:
```python
import math

import jax
import jax.numpy as jnp
from jax import lax
from jax.sharding import PartitionSpec as P

D = 8192
HEADS = 32
KV_HEADS = 4
HEAD = 128
TILE = 128


def slot_table(tile_of_slot, tile_count):
    numbers = jnp.arange(tile_count, dtype=jnp.int32)
    matches = tile_of_slot[None, :] == numbers[:, None]
    return jnp.sum(jnp.where(matches, numbers[None, :], 0), axis=1)


def live_slots(ancestors, slot_of, own_slots, tile_count):
    numbers = jnp.arange(tile_count, dtype=jnp.int32)
    matches = ancestors[:, :, None] == numbers[None, None, :]
    located = jnp.sum(jnp.where(matches, slot_of[None, None, :], 0), axis=2)
    located = jnp.where(ancestors >= 0, located, -1)
    width_anc = ancestors.shape[1]
    before = jnp.arange(width_anc)[:, None] > jnp.arange(width_anc)[None, :]
    repeated = jnp.any((located[:, :, None] == located[:, None, :]) & before[None], axis=2)
    keeping = (located >= 0) & (located != own_slots[:, None]) & jnp.logical_not(repeated)
    return jnp.where(keeping, located, -1)


def body(query, keys_values, ancestors, tile_of_slot, residual, norm_gain, out_weight):
    tiles_here = query.shape[0] // TILE
    heads_here = query.shape[1] // HEAD
    group_full = HEADS // KV_HEADS
    kv_here = max(1, heads_here // group_full)
    group_size = heads_here // kv_here
    kv_first = lax.axis_index("mp") * heads_here // group_full
    local_pairs = lax.dynamic_slice_in_dim(keys_values, kv_first * HEAD, kv_here * HEAD, 2)
    dp_count = lax.axis_size("dp")
    dp_index = lax.axis_index("dp")
    tile_count = tiles_here * dp_count
    score_scale = HEAD ** (-0.5)
    slot_of = slot_table(tile_of_slot, tile_count)
    own_slots = dp_index * tiles_here + jnp.arange(tiles_here, dtype=jnp.int32)
    far_slots = live_slots(ancestors, slot_of, own_slots, tile_count)
    query_grid = query.reshape(tiles_here, TILE, kv_here, group_size, HEAD)
    own_keys = local_pairs[0].reshape(tiles_here, TILE, kv_here, HEAD)
    own_values = local_pairs[1].reshape(tiles_here, TILE, kv_here, HEAD)
    near = (
        jnp.einsum("tqhgd,tkhd->thgqk", query_grid, own_keys, preferred_element_type=jnp.float32)
        * score_scale
    )
    causal = jnp.arange(TILE)[:, None] >= jnp.arange(TILE)[None, :]
    near = jnp.where(causal, near, -jnp.inf)
    peak_start = jnp.max(near, axis=4)
    near_weight = jnp.exp(near - peak_start[..., None])
    totals_start = jnp.sum(near_weight, axis=4)
    accum_start = jnp.einsum(
        "thgqk,tkhd->thgqd",
        near_weight.astype(jnp.bfloat16),
        own_values,
        preferred_element_type=jnp.float32,
    )
    running = (peak_start, totals_start, accum_start)

    def absorb(state, key_tiles, value_tiles, key_slots):
        peak_old, totals_old, accum_old = state
        visible = (
            jnp.any(far_slots[:, :, None] == key_slots[None, None, :], axis=1)
            & (key_slots >= 0)[None, :]
        )
        scores = (
            jnp.einsum(
                "tqhgd,nkhd->thgqnk", query_grid, key_tiles, preferred_element_type=jnp.float32
            )
            * score_scale
        )
        scores = jnp.where(visible[:, None, None, None, :, None], scores, -jnp.inf)
        peak_new = jnp.maximum(peak_old, jnp.max(scores, axis=(4, 5)))
        weights = jnp.exp(scores - peak_new[..., None, None])
        rescale = jnp.exp(peak_old - peak_new)
        totals_new = totals_old * rescale + jnp.sum(weights, axis=(4, 5))
        accum_new = accum_old * rescale[..., None] + jnp.einsum(
            "thgqnk,nkhd->thgqd",
            weights.astype(jnp.bfloat16),
            value_tiles,
            preferred_element_type=jnp.float32,
        )
        return (peak_new, totals_new, accum_new)

    piece_pair = lax.all_gather(local_pairs, "dp", axis=1, tiled=True)
    piece_tiles = piece_pair.shape[1] // TILE
    key_tiles = piece_pair[0].reshape(piece_tiles, TILE, kv_here, HEAD)
    value_tiles = piece_pair[1].reshape(piece_tiles, TILE, kv_here, HEAD)
    key_slots = jnp.arange(piece_tiles)
    tile_total = key_tiles.shape[0]
    block_size = math.gcd(tile_total, 8)
    blocks = tile_total // block_size
    key_blocks = key_tiles.reshape(blocks, block_size, TILE, kv_here, HEAD)
    value_blocks = value_tiles.reshape(blocks, block_size, TILE, kv_here, HEAD)
    slot_blocks = key_slots.reshape(blocks, block_size)

    def absorb_block(current, bundle):
        return (absorb(current, bundle[0], bundle[1], bundle[2]), None)

    result, _ = lax.scan(absorb_block, running, (key_blocks, value_blocks, slot_blocks))
    running = result
    peak_end, totals_end, accum_end = running
    mixed = accum_end / totals_end[..., None]
    attended = (
        jnp.transpose(mixed, (0, 3, 1, 2, 4))
        .reshape(tiles_here * TILE, query.shape[1])
        .astype(jnp.bfloat16)
    )
    term = jnp.dot(attended, out_weight, preferred_element_type=jnp.float32)
    share_sum = lax.psum_scatter(
        term.astype(jnp.bfloat16), "mp", scatter_dimension=1, tiled=True
    ).astype(jnp.float32)
    hidden_out = (residual.astype(jnp.float32) + share_sum).astype(jnp.bfloat16)
    hidden_f32 = hidden_out.astype(jnp.float32)
    squares = lax.psum(jnp.sum(hidden_f32 * hidden_f32, axis=1), "mp")
    mean_sq = squares / D
    normed = hidden_f32 * lax.rsqrt(mean_sq + 1e-05)[:, None] * norm_gain[None, :]
    return (hidden_out, normed.astype(jnp.bfloat16))


def solution(mesh):
    return jax.shard_map(
        body,
        mesh=mesh,
        in_specs=(
            P("dp", "mp"),
            P(None, "dp", None),
            P("dp", None),
            P(),
            P("dp", "mp"),
            P("mp"),
            P("mp", None),
        ),
        out_specs=(P("dp", "mp"), P("dp", "mp")),
        check_vma=False,
    )
```

profile of v0, /device:TPU:0, one launch (start us, length us, event | category | flops | bytes accessed | tf_op | source)
XLA Modules:
  0.0 137.6 jit_solution(16881295355535212365)
XLA Ops:
  7.2 0.0 all-gather.2.cloned.1.call-start
  7.2 1.6 %constant_dynamic-slice_fusion.3 = bf16[2,256,128]{2,1,0:T(8,128)(2,1)} fusion(bf16[2,256,512]{2,1,0:T(8,128)(2,1)} %param.10, s32[]{:T(128)S(6)} %select_n.32), kind=kLoop, calls=%fused_computation.63 | loop fusion | bytes 262148 | tf_op jit(solution)/shard_map/dynamic_slice | solution.py:40
  8.8 0.0 all-gather.2.cloned.1.call-update
  8.8 0.0 reduce-scatter.2.cloned.1.call-start
  8.9 0.7 broadcast_compare_fusion
  9.6 0.8 select_reduce_fusion
  10.3 0.8 copy.26
  11.1 1.1 copy.53
  12.2 0.1 copy.27
  12.4 0.3 fusion.39
  12.7 0.1 copy.28
  12.8 0.2 and_reduce_fusion
  13.0 0.1 copy.30
  13.1 0.1 copy.32
  13.2 0.1 copy.34
  13.4 0.9 constant_dynamic-slice_fusion.2
  14.3 0.3 fusion.41
  14.6 0.4 convolution_bitcast_fusion
  14.9 0.2 fusion.31
  15.1 38.6 %all-gather.2.cloned.1.call-done = bf16[2,2048,128]{2,1,0:T(8,128)(2,1)} async-done(((bf16[2,256,128]{2,1,0:T(8,128)(2,1)}), bf16[2,2048,128]{2,1,0:T(8,128)(2,1)}) %all-gather.2.cloned.1.call-update) | async-done | bytes 1048592 | tf_op jit(solution)/shard_map/all_gather | solution.py:93
  53.7 1.3 fusion.40
  55.0 11.1 %while.14 = (s32[]{:T(128)}, f32[2,1,8,128]{3,2,0,1:T(8,128)S(1)}, f32[2,1,8,128]{3,2,0,1:T(8,128)S(1)}, f32[2,1,8,128,128]{3,4,2,0,1:T(8,128)S(1)}, s32[2,12]{1...) while((s32[]{:T(128)}, f32[2,1,8,128]{3,2,0,1:T(8,128)S(1)}, ...), condition=%wide.region_9.10_spmd, body=%wide.region_5.9_spmd.sunk | while | flops 1097341312 | bytes 28445124 | solution.py:108
  55.0 0.2 compare_reduce_fusion.2
  55.2 0.1 copy.65
  55.3 1.3 fusion.55
  56.6 2.2 %fusion.58 = f32[2,1,8,128,128]{3,4,2,0,1:T(8,128)S(1)} fusion(f32[8,128,2,128,8]{3,1,4,2,0:T(8,128)S(1)} %get-tuple-element.170, f32[2,8,128]{2,1,0:T(8,128)S(1)} %bitcast.147, pred[2,8]{0,1:T(8,128)(4,1)S(1)} %copy.65, f32[2,1,8,128,128]{3,4,2,0,1:T(8,128)S(1)} %get-tuple-element.185, f32[2,8,128]{2,1,0:T(8,128)S(1)} %get-tuple-element.171, ...), kind=kOutput, calls=%fused_computation.9.clone.1 | convolution fusion | flops 545783808 | bytes 10765316 | tf_op jit(solution)/shard_map/while/body/eval_jaxpr/thgqnk,nkhd->thgqd/dot_general | solution.py:85
  58.8 1.7 %fusion.57 = f32[2,8,128]{2,1,0:T(8,128)S(1)} fusion(f32[8,128,2,128,8]{3,1,4,2,0:T(8,128)S(1)} %get-tuple-element.170, f32[2,8,128]{2,1,0:T(8,128)S(1)} %bitcast.148, pred[2,8]{0,1:T(8,128)(4,1)S(1)} %copy.65), kind=kLoop, calls=%fused_computation.3.clone.1 | loop fusion | flops 8386560 | bytes 8405008 | tf_op jit(solution)/shard_map/while/body/eval_jaxpr/reduce_sum | solution.py:84
  60.5 0.2 compare_reduce_fusion.2
  60.8 0.1 copy.65
  60.8 1.3 fusion.55
  62.1 2.2 %fusion.58 = f32[2,1,8,128,128]{3,4,2,0,1:T(8,128)S(1)} fusion(f32[8,128,2,128,8]{3,1,4,2,0:T(8,128)S(1)} %get-tuple-element.170, f32[2,8,128]{2,1,0:T(8,128)S(1)} %bitcast.147, pred[2,8]{0,1:T(8,128)(4,1)S(1)} %copy.65, f32[2,1,8,128,128]{3,4,2,0,1:T(8,128)S(1)} %get-tuple-element.185, f32[2,8,128]{2,1,0:T(8,128)S(1)} %get-tuple-element.171, ...), kind=kOutput, calls=%fused_computation.9.clone.1 | convolution fusion | flops 545783808 | bytes 10765316 | tf_op jit(solution)/shard_map/while/body/eval_jaxpr/thgqnk,nkhd->thgqd/dot_general | solution.py:85
  64.3 1.7 %fusion.57 = f32[2,8,128]{2,1,0:T(8,128)S(1)} fusion(f32[8,128,2,128,8]{3,1,4,2,0:T(8,128)S(1)} %get-tuple-element.170, f32[2,8,128]{2,1,0:T(8,128)S(1)} %bitcast.148, pred[2,8]{0,1:T(8,128)(4,1)S(1)} %copy.65), kind=kLoop, calls=%fused_computation.3.clone.1 | loop fusion | flops 8386560 | bytes 8405008 | tf_op jit(solution)/shard_map/while/body/eval_jaxpr/reduce_sum | solution.py:84
  66.1 0.1 fusion.38
  66.2 0.3 copy.36
  66.5 0.0 copy-start.1
  66.5 0.0 copy-start.2
  66.6 11.9 %convolution_convert_fusion = bf16[256,8192]{1,0:T(8,128)(2,1)} fusion(bf16[1024,8192]{1,0:T(8,128)(2,1)} %param.15, bf16[32,8,8,128]{3,2,1,0:T(8,128)(2,1)S(1)} %bitcast.151), kind=kOutput, calls=%fused_computation.29 | convolution fusion | flops 4297064448 | bytes 21495808 | tf_op jit(solution)/shard_map/dot_general | solution.py:117
  78.4 0.0 reduce-scatter.2.cloned.1.call-update
  78.5 43.4 %reduce-scatter.2.cloned.1.call-done = bf16[256,2048]{1,0:T(8,128)(2,1)} async-done(((bf16[256,8192]{1,0:T(8,128)(2,1)}), bf16[256,2048]{1,0:T(8,128)(2,1)}) %reduce-scatter.2.cloned.1.call-update) | async-done | bytes 1048592 | tf_op jit(solution)/shard_map/reduce_scatter | solution.py:118
  121.9 0.0 copy-done.1
  121.9 1.7 %fusion.25 = (f32[256]{0:T(256)S(1)}, bf16[256,2048]{1,0:T(8,128)(2,1)S(1)}) fusion(bf16[256,2048]{1,0:T(8,128)(2,1)} %reduce-scatter.2.cloned.1.call-done, bf16[256,2048]{1,0:T(8,128)(2,1)S(1)} %copy-done.1), kind=kLoop, calls=%fused_computation.32 | loop fusion | flops 3669760 | bytes 3146752 | tf_op jit(solution)/shard_map/reduce_sum | solution.py:123
  123.7 0.0 copy-start
  123.7 5.8 %psum.7 = f32[256]{0:T(256)S(1)} all-reduce(f32[256]{0:T(256)S(1)} %get-tuple-element.99), channel_id=1, replica_groups=mesh['dp'=8,'mp'=4] {'mp'}, use_global_device_ids=true, to_apply=%region_12.13 | all-reduce | flops 256 | bytes 2048 | tf_op jit(solution)/shard_map/psum | solution.py:123
  129.4 0.0 copy-done.2
  129.4 1.3 fusion.27
  130.7 0.0 copy-done
  (19 shorter events, 0.1 us)
Async XLA Ops:
  7.2 46.5 %all-gather.2.cloned.1.call-start = ((), (), s32[]{:S(2)}) async-start(), calls=%async_computation.1 | async-start | bytes 1179648 | tf_op jit(solution)/shard_map/all_gather | solution.py:93
  8.8 113.1 %reduce-scatter.2.cloned.1.call-start = ((), (), s32[]{:S(2)}) async-start(), calls=%async_computation.2 | async-start | bytes 5242880 | tf_op jit(solution)/shard_map/reduce_scatter | solution.py:118
  66.5 55.4 %copy-start.1 = (bf16[256,2048]{1,0:T(8,128)(2,1)S(1)}, bf16[256,2048]{1,0:T(8,128)(2,1)}, u32[]{:S(2)}) copy-start(bf16[256,2048]{1,0:T(8,128)(2,1)} %param.13) | copy-start | bytes 3145732
  66.5 62.9 %copy-start.2 = (f32[2048]{0:T(1024)S(1)}, f32[2048]{0:T(1024)}, u32[]{:S(2)}) copy-start(f32[2048]{0:T(1024)} %param.14) | copy-start | bytes 24580
  123.7 7.1 %copy-start = (bf16[256,2048]{1,0:T(8,128)(2,1)}, bf16[256,2048]{1,0:T(8,128)(2,1)S(1)}, u32[]{:S(2)}) copy-start(bf16[256,2048]{1,0:T(8,128)(2,1)S(1)} %get-tuple-element.100) | copy-start | bytes 3145732
Sparse Core Ops, SparseCore 0:
  10.8 42.8 all-gather.1
  78.6 43.2 reduce-scatter.1
where the time goes:
time: 138 us
  waiting for transfers between devices  82 us (59%)
  matrix products  19.5 us (14%)
  between operations  14.2 us (10%)
  other arithmetic  9.21 us (7%)
  local copies, waits for them, and re-layouts  6.67 us (5%)
  blocking collectives  5.76 us (4%)
    reduce_scatter x1, waiting for transfers between devices, body(): lax.psum_scatter(term.astype(jnp.bfloat16), 'mp', scatter_dimension=1, ti...  43.4 us
    all_gather x1, waiting for transfers between devices, body(): piece_pair = lax.all_gather(local_pairs, 'dp', axis=1, tiled=True)  38.6 us
    dot_general x1, matrix products, body(): term = jnp.dot(attended, out_weight, preferred_element_type=jnp.float32)  11.9 us
    psum x1, blocking collectives, body(): squares = lax.psum(jnp.sum(hidden_f32 * hidden_f32, axis=1), 'mp')  5.76 us
    dot_general x2, matrix products, absorb(): jnp.einsum('thgqnk,nkhd->thgqd', weights.astype(jnp.bfloat16), value_tile...  4.41 us
    reduce_sum x2, other arithmetic, absorb(): totals_new = totals_old * rescale + jnp.sum(weights, axis=(4, 5))  3.4 us
  transfers between devices with their start and end apart: 2, of which 2 were waited for; matrix products, arithmetic and copies ran while one was open for 4% of the time, Pallas kernels for 0%

commit v1 on v0

v1 whole, which is shorter than its diff:
```python
import functools
import math

import jax
import jax.numpy as jnp
from jax import lax
from jax.experimental import pallas as pl
from jax.experimental.pallas import tpu as pltpu
from jax.sharding import PartitionSpec as P

HEAD = 128
TILE = 128
WIDTH = 512
F32 = jnp.float32
BF16 = jnp.bfloat16
MESH = pl.DeviceIdType.MESH


def kernel(
    sizes,
    anc_ref, slots_ref, query_ref, pairs_ref, residual_ref, gain_ref, weight_ref,
    hidden_ref, normed_ref,
    kv, keys, values, bias, q, res, gain, w, att, near_send, near_recv,
    far_send, far_recv, own, hid, nrm, sq_send, sq_recv,
    load_sem, w_sem, out_sem, kv_recv_sem, kv_z_sem, kv_x_sem,
    near_send_sem, near_recv_sem, far_send_sem, far_recv_sem, sq_send_sem, sq_recv_sem,
):
    dp_count, mp_count, nx, tiles, heads, kv_heads, width = sizes
    nz = dp_count // nx
    ny = mp_count // 2
    features = mp_count * width
    chunks = width // WIDTH
    me_dp, me_mp = lax.axis_index("dp"), lax.axis_index("mp")
    z, x = me_dp // nx, me_dp % nx
    y, core = me_mp // 2, me_mp % 2
    sibling = y * 2 + (1 - core)

    def dev(dp, mp):
        return {"dp": dp, "mp": mp}

    kv_head = me_mp * kv_heads // mp_count
    own_kv = pltpu.make_async_copy(
        pairs_ref.at[:, :, pl.ds(pl.multiple_of(kv_head * HEAD, HEAD), HEAD)],
        kv.at[me_dp], load_sem.at[0])
    own_kv.start()
    load_q = pltpu.make_async_copy(query_ref, q, load_sem.at[1])
    load_q.start()
    blocks = []
    for dy in list(range(1, ny)) + [0]:
        for other in (1, 0):
            block = ((y + dy) % ny) * 2 + (core if other == 0 else 1 - core)
            blocks.append(block)
    w_loads = []
    for i, block in enumerate(blocks):
        copy = pltpu.make_async_copy(
            weight_ref.at[:, pl.ds(pl.multiple_of(block * width, width), width)],
            w.at[i], w_sem.at[i])
        copy.start()
        w_loads.append(copy)
    load_res = pltpu.make_async_copy(residual_ref, res, load_sem.at[2])
    load_res.start()
    load_gain = pltpu.make_async_copy(gain_ref, gain, load_sem.at[3])
    load_gain.start()

    barrier = pltpu.get_barrier_semaphore()
    for dm in range(1, mp_count):
        pl.semaphore_signal(barrier, inc=1, device_id=dev(me_dp, (me_mp + dm) % mp_count), device_id_type=MESH)
    for dx in range(1, nx):
        pl.semaphore_signal(barrier, inc=1, device_id=dev(z * nx + (x + dx) % nx, me_mp), device_id_type=MESH)

    @pl.when(z > 0)
    def _():
        pl.semaphore_signal(barrier, inc=1, device_id=dev(me_dp - nx, me_mp), device_id_type=MESH)

    @pl.when(z < nz - 1)
    def _():
        pl.semaphore_signal(barrier, inc=1, device_id=dev(me_dp + nx, me_mp), device_id_type=MESH)

    ends = jnp.where(z > 0, 1, 0) + jnp.where(z < nz - 1, 1, 0)
    pl.semaphore_wait(barrier, mp_count - 1 + nx - 1 + ends)
    own_kv.wait()

    def kv_copy(src, target, send_sem):
        return pltpu.make_async_remote_copy(
            src_ref=kv.at[src], dst_ref=kv.at[src], send_sem=send_sem,
            recv_sem=kv_recv_sem.at[src], device_id=dev(target, me_mp), device_id_type=MESH)

    def z_send(line, up):
        return kv_copy(line * nx + x, me_dp + (nx if up else -nx), kv_z_sem.at[1 if up else 0, line])

    def x_send(line, dx):
        return kv_copy(line * nx + x, z * nx + (x + dx) % nx, kv_x_sem.at[dx - 1, line])

    @pl.when(z < nz - 1)
    def _():
        z_send(z, True).start()

    @pl.when(z > 0)
    def _():
        z_send(z, False).start()

    for dx in range(1, nx):
        x_send(z, dx).start()

    for t in range(tiles):
        bias[t, :, 0:TILE] = jnp.zeros((8, TILE), F32)

    def lookup(src, picks):
        seen = []
        for t in range(tiles):
            row = []
            for u in range(tiles):
                slot = src * tiles + u
                tile_id = slots_ref[slot]
                found = jnp.int32(0)
                for j in range(anc_ref.shape[1]):
                    found = found | jnp.where(anc_ref[t, j] == tile_id, 1, 0)
                found = found * jnp.where(slot == me_dp * tiles + t, 0, 1)
                row.append(found)
            seen.append(row)
        for t in range(tiles):
            hit = functools.reduce(lambda a, b: a | b, seen[t])
            column = jnp.where(jnp.full((8, TILE), hit) > 0, 0.0, -jnp.inf).astype(F32)
            bias[t, :, pl.ds(pl.multiple_of((src + 1) * TILE, TILE), TILE)] = column
        return tuple(
            tuple(jnp.where(i == src, functools.reduce(lambda a, b: a | b, [seen[t][u] for t in range(tiles)]), old)
                  for i, old in enumerate(picks[u]))
            for u in range(tiles))

    picks = lax.fori_loop(
        0, dp_count, lookup,
        tuple(tuple(jnp.int32(0) for _ in range(dp_count)) for _ in range(tiles)))

    for d in range(1, nz):
        @pl.when(z >= d)
        def _():
            line = z - d
            kv_copy(line * nx + x, me_dp, kv_z_sem.at[0, 0]).wait_recv()

            @pl.when(z < nz - 1)
            def _():
                z_send(line, True).start()

            for dx in range(1, nx):
                x_send(line, dx).start()

        @pl.when(z + d < nz)
        def _():
            line = z + d
            kv_copy(line * nx + x, me_dp, kv_z_sem.at[0, 0]).wait_recv()

            @pl.when(z > 0)
            def _():
                z_send(line, False).start()

            for dx in range(1, nx):
                x_send(line, dx).start()

    load_q.wait()
    for dx in range(1, nx):
        for line in range(nz):
            kv_copy(line * nx + (x + dx) % nx, me_dp, kv_z_sem.at[0, 0]).wait_recv()

    for src in range(dp_count):
        for half, target in ((0, keys), (1, values)):
            best = kv[src, half, 0:TILE, :]
            for u in range(1, tiles):
                wanted = jnp.full((TILE, HEAD), picks[u][src]) > 0
                best = jnp.where(wanted, kv[src, half, u * TILE:(u + 1) * TILE, :].astype(F32), best.astype(F32)).astype(BF16)
            for t in range(tiles):
                target[t, (src + 1) * TILE:(src + 2) * TILE, :] = best
    for t in range(tiles):
        for half, target in ((0, keys), (1, values)):
            target[t, 0:TILE, :] = kv[me_dp, half, t * TILE:(t + 1) * TILE, :]

    pair = 2 if heads % 2 == 0 else 1
    exponent = HEAD ** (-0.5) * math.log2(math.e)
    causal = (
        lax.broadcasted_iota(jnp.int32, (TILE, TILE), 0)
        >= lax.broadcasted_iota(jnp.int32, (TILE, TILE), 1)
    )
    causal = jnp.concatenate([causal] * pair, axis=0)

    def attention(t):
        rows = slice(t * TILE, (t + 1) * TILE)

        def step(hp, carry):
            columns = pl.ds(pl.multiple_of(hp * (pair * HEAD), pair * HEAD), pair * HEAD)
            both = q[rows, columns]
            stacked = jnp.concatenate([both[:, i * HEAD:(i + 1) * HEAD] for i in range(pair)], axis=0)
            scores = lax.dot_general(stacked, keys[t], (((1,), (1,)), ((), ())), preferred_element_type=F32)
            near = jnp.where(causal, scores[:, :TILE], -jnp.inf)
            scores = jnp.concatenate([near, scores[:, TILE:] + bias[t, 0:1, TILE:]], axis=1)
            peak = jnp.max(scores, axis=1, keepdims=True)
            weights = jnp.exp2((scores - peak) * exponent)
            totals = jnp.sum(weights, axis=1, keepdims=True)
            mixed = jnp.dot(weights.astype(BF16), values[t], preferred_element_type=F32) / totals
            mixed = mixed.astype(BF16)
            att[rows, columns] = jnp.concatenate([mixed[i * TILE:(i + 1) * TILE] for i in range(pair)], axis=1)
            return carry

        lax.fori_loop(0, heads // pair, step, 0)

    def project(t, i, j):
        return jnp.dot(att[t * TILE:(t + 1) * TILE, :], w[i, :, j * WIDTH:(j + 1) * WIDTH], preferred_element_type=F32)

    def near_copy(t, dy, j):
        return pltpu.make_async_remote_copy(
            src_ref=near_send.at[dy, t, j], dst_ref=near_recv.at[dy, t, j],
            send_sem=near_send_sem.at[dy, t, j], recv_sem=near_recv_sem.at[dy, t, j],
            device_id=dev(me_dp, sibling), device_id_type=MESH)

    def far_copy(t, dy, j):
        return pltpu.make_async_remote_copy(
            src_ref=far_send.at[dy - 1, t, j], dst_ref=far_recv.at[dy - 1, t, j],
            send_sem=far_send_sem.at[dy - 1, t, j], recv_sem=far_recv_sem.at[dy - 1, t, j],
            device_id=dev(me_dp, ((y + dy) % ny) * 2 + core), device_id_type=MESH)

    def sq_copy(t, dm):
        return pltpu.make_async_remote_copy(
            src_ref=sq_send.at[t], dst_ref=sq_recv.at[t, dm - 1],
            send_sem=sq_send_sem.at[t, dm - 1], recv_sem=sq_recv_sem.at[t, dm - 1],
            device_id=dev(me_dp, (me_mp + dm) % mp_count), device_id_type=MESH)

    def give(t, dy, j):
        i = 2 * ((dy - 1) % ny)
        near_send[dy, t, j] = project(t, i, j).astype(BF16)
        near_copy(t, dy, j).start()

    def take(t, dy, j):
        i = 2 * ((dy - 1) % ny) + 1
        part = project(t, i, j)
        if dy == 0:
            own[t, j] = part
            return
        near_copy(t, dy, j).wait_recv()
        far_send[dy - 1, t, j] = (part + near_recv[dy, t, j].astype(F32)).astype(BF16)
        far_copy(t, dy, j).start()

    def run(t, dys):
        work = [(dy, j) for dy in dys for j in range(chunks)]
        for n in range(len(work) + 1):
            if n < len(work):
                give(t, *work[n])
            if n > 0:
                take(t, *work[n - 1])

    far_dys = list(range(1, ny))
    for t in range(tiles):
        attention(t)
        if t == 0:
            for copy in w_loads:
                copy.wait()
        run(t, far_dys)
    for t in range(tiles):
        run(t, [0])

    load_res.wait()
    load_gain.wait()

    def gather(t):
        rows = slice(t * TILE, (t + 1) * TILE)
        square = jnp.zeros((TILE, HEAD), F32)
        for j in range(chunks):
            near_copy(t, 0, j).wait_recv()
            for dy in far_dys:
                far_copy(t, dy, j).wait_recv()
            total = own[t, j] + near_recv[0, t, j].astype(F32)
            for dy in far_dys:
                total = total + far_recv[dy - 1, t, j].astype(F32)
            columns = slice(j * WIDTH, (j + 1) * WIDTH)
            out = (res[rows, columns].astype(F32) + total).astype(BF16)
            hid[rows, columns] = out
            out = out.astype(F32)
            out = out * out
            for k in range(WIDTH // HEAD):
                square = square + out[:, k * HEAD:(k + 1) * HEAD]
        line = jnp.broadcast_to(jnp.sum(square, axis=1, keepdims=True), (TILE, TILE))
        sq_send[t] = jnp.transpose(line)[0:8, :]
        for dm in range(1, mp_count):
            sq_copy(t, dm).start()
        pltpu.make_async_copy(hid.at[pl.ds(t * TILE, TILE)], hidden_ref.at[pl.ds(t * TILE, TILE)], out_sem.at[0, t]).start()

    def finish(t):
        rows = slice(t * TILE, (t + 1) * TILE)
        total = sq_send[t]
        for dm in range(1, mp_count):
            sq_copy(t, dm).wait_recv()
            total = total + sq_recv[t, dm - 1]
        line = lax.rsqrt(total[0:1, :] / features + 1e-05)
        scale = jnp.transpose(jnp.broadcast_to(line, (TILE, TILE)))
        for k in range(width // HEAD):
            columns = slice(k * HEAD, (k + 1) * HEAD)
            nrm[rows, columns] = (hid[rows, columns].astype(F32) * scale * gain[0:1, columns]).astype(BF16)
        pltpu.make_async_copy(nrm.at[pl.ds(t * TILE, TILE)], normed_ref.at[pl.ds(t * TILE, TILE)], out_sem.at[1, t]).start()

    for t in range(tiles):
        gather(t)
        if t > 0:
            finish(t - 1)

    for line in range(nz):
        @pl.when((z < nz - 1) & (z >= line))
        def _():
            z_send(line, True).wait_send()

        @pl.when((z > 0) & (z <= line))
        def _():
            z_send(line, False).wait_send()

        for dx in range(1, nx):
            x_send(line, dx).wait_send()
    for t in range(tiles):
        for j in range(chunks):
            for dy in range(ny):
                near_copy(t, dy, j).wait_send()
            for dy in far_dys:
                far_copy(t, dy, j).wait_send()
    finish(tiles - 1)
    for t in range(tiles):
        for dm in range(1, mp_count):
            sq_copy(t, dm).wait_send()
        pltpu.make_async_copy(hid.at[pl.ds(t * TILE, TILE)], hidden_ref.at[pl.ds(t * TILE, TILE)], out_sem.at[0, t]).wait()
        pltpu.make_async_copy(nrm.at[pl.ds(t * TILE, TILE)], normed_ref.at[pl.ds(t * TILE, TILE)], out_sem.at[1, t]).wait()


def solution(mesh):
    dp_count, mp_count = mesh.shape["dp"], mesh.shape["mp"]
    nx = 2 ** (int(math.log2(dp_count)) // 2)
    if dp_count % nx:
        nx = 1
    ny = mp_count // 2

    def body(query, keys_values, ancestors, tile_of_slot, residual, norm_gain, out_weight):
        tokens, inner = query.shape
        tiles, heads = tokens // TILE, inner // HEAD
        width = residual.shape[1]
        kv_heads = keys_values.shape[2] // HEAD
        chunks = width // WIDTH
        sizes = (dp_count, mp_count, nx, tiles, heads, kv_heads, width)
        dma = pltpu.SemaphoreType.DMA
        anywhere = pl.BlockSpec(memory_space=pl.ANY)
        smem = pl.BlockSpec(memory_space=pltpu.SMEM)
        span = (dp_count + 1) * TILE
        nz = dp_count // nx
        fy = max(ny - 1, 1)
        return pl.pallas_call(
            functools.partial(kernel, sizes),
            out_shape=(jax.ShapeDtypeStruct(residual.shape, BF16),) * 2,
            in_specs=[smem, smem] + [anywhere] * 5,
            out_specs=(anywhere, anywhere),
            scratch_shapes=[
                pltpu.VMEM((dp_count, 2, tokens, HEAD), BF16),
                pltpu.VMEM((tiles, span, HEAD), BF16),
                pltpu.VMEM((tiles, span, HEAD), BF16),
                pltpu.VMEM((tiles, 8, span), F32),
                pltpu.VMEM((tokens, inner), BF16),
                pltpu.VMEM((tokens, width), BF16),
                pltpu.VMEM((1, width), F32),
                pltpu.VMEM((mp_count, inner, width), BF16),
                pltpu.VMEM((tokens, inner), BF16),
                pltpu.VMEM((ny, tiles, chunks, TILE, WIDTH), BF16),
                pltpu.VMEM((ny, tiles, chunks, TILE, WIDTH), BF16),
                pltpu.VMEM((fy, tiles, chunks, TILE, WIDTH), BF16),
                pltpu.VMEM((fy, tiles, chunks, TILE, WIDTH), BF16),
                pltpu.VMEM((tiles, chunks, TILE, WIDTH), F32),
                pltpu.VMEM((tokens, width), BF16),
                pltpu.VMEM((tokens, width), BF16),
                pltpu.VMEM((tiles, 8, TILE), F32),
                pltpu.VMEM((tiles, mp_count - 1, 8, TILE), F32),
                dma((4,)), dma((mp_count,)), dma((2, tiles)),
                dma((dp_count,)), dma((2, nz)), dma((max(nx - 1, 1), nz)),
                dma((ny, tiles, chunks)), dma((ny, tiles, chunks)),
                dma((fy, tiles, chunks)), dma((fy, tiles, chunks)),
                dma((tiles, mp_count - 1)), dma((tiles, mp_count - 1)),
            ],
            compiler_params=pltpu.CompilerParams(
                collective_id=0, has_side_effects=True, vmem_limit_bytes=56 * 1024 * 1024),
        )(ancestors, tile_of_slot, query, keys_values, residual, norm_gain.reshape(1, width), out_weight)

    return jax.shard_map(
        body,
        mesh=mesh,
        in_specs=(
            P("dp", "mp"),
            P(None, "dp", None),
            P("dp", None),
            P(),
            P("dp", "mp"),
            P("mp"),
            P("mp", None),
        ),
        out_specs=(P("dp", "mp"), P("dp", "mp")),
        check_vma=False,
    )
```

time: 138 us -> 62.4 us (0.45)
  waiting for transfers between devices: 82 us -> 0 us
  Pallas kernels: 0 us -> 56.9 us
  matrix products: 19.5 us -> 0 us
  between operations: 14.2 us -> 0.64 us
  other arithmetic: 9.21 us -> 0 us
  blocking collectives: 5.76 us -> 0 us
  local copies, waits for them, and re-layouts: 6.67 us -> 4.61 us
    pallas_call x0 -> x1, Pallas kernels: none -> 56.9 us  [body(): pl.pallas_call(functools.partial(kernel, sizes), out_shape=(jax.ShapeDtyp...]
    reduce_scatter x1 -> x0, waiting for transfers between devices: 43.4 us -> none  [body(): lax.psum_scatter(term.astype(jnp.bfloat16), 'mp', scatter_dimension=1, ti...]
    all_gather x1 -> x0, waiting for transfers between devices: 38.6 us -> none  [body(): piece_pair = lax.all_gather(local_pairs, 'dp', axis=1, tiled=True)]
    dot_general x7 -> x0, matrix products: 19.5 us -> none  [the longest x1 11.9 us: body(): term = jnp.dot(attended, out_weight, preferred_element_type=jnp.float32)]
    reduce_sum x6 -> x0, other arithmetic: 6.43 us -> none  [the longest x2 3.4 us: absorb(): totals_new = totals_old * rescale + jnp.sum(weights, axis=(4, 5))]
    psum x1 -> x0, blocking collectives: 5.76 us -> none  [body(): squares = lax.psum(jnp.sum(hidden_f32 * hidden_f32, axis=1), 'mp')]
    unnamed x8 -> x2, local copies, waits for them, and re-layouts: 1.92 us -> 4.61 us
    slice x2 -> x0, local copies, waits for them, and re-layouts: 2.16 us -> none  [the longest x1 1.27 us: body(): value_tiles = piece_pair[1].reshape(piece_tiles, TILE, kv_here, HEAD)]
  transfers between devices with their start and end apart: 2 -> 0, of which waited for: 2 -> 0; matrix products, arithmetic and copies ran while one was open for 4% -> 0% of each run, Pallas kernels for 0% -> 0%
where the time goes in v1:
time: 62.4 us; the launch traced here: 62.2 us
  Pallas kernels  56.9 us (91%)
  local copies, waits for them, and re-layouts  4.61 us (7%)
  between operations  0.64 us (1%)
    pallas_call x1, Pallas kernels, body(): pl.pallas_call(functools.partial(kernel, sizes), out_shape=(jax.ShapeDtyp...  56.9 us
    unnamed x2, local copies, waits for them, and re-layouts  4.61 us

profile of v1, /device:TPU:0, one launch (start us, length us, event | category | flops | bytes accessed | tf_op | source)
XLA Modules:
  0.0 62.2 jit_solution(335581260835529088)
XLA Ops:
  0.6 56.9 %shard_map.86 = (bf16[256,2048]{1,0:T(8,128)(2,1)}, bf16[256,2048]{1,0:T(8,128)(2,1)}) custom-call(s32[2,12]{1,0:T(2,128)} %anc_ref.1, s32[16]{0:T(128)} %slots_ref.1, bf16[256,1024]{1,0:T(8,128)(2,1)} %query_ref.1, bf16[2,256,512]{2,1,0:T(8,128)(2,1)} %pairs_ref.1, bf16[256,2048]{1,0:T(8,128)(2,1)} %residual_ref.1, f32[1,2048]{1,0:T(1,128)} %bitcast.1, ...), custom_call_target="tpu_custom_call" | custom-call | tf_op jit(solution)/shard_map/pallas_call | solution.py:347
  57.6 2.3 %copy.11 = bf16[256,2048]{1,0:T(8,128)(2,1)} copy(bf16[256,2048]{1,0:T(8,128)(2,1)} %get-tuple-element.4) | data formatting | bytes 2097152
  59.9 2.3 %copy.12 = bf16[256,2048]{1,0:T(8,128)(2,1)} copy(bf16[256,2048]{1,0:T(8,128)(2,1)} %get-tuple-element.5) | data formatting | bytes 2097152

commit v2 on v1

v2 whole, which is shorter than its diff:
```python
import functools
import math

import jax
import jax.numpy as jnp
from jax import lax
from jax.experimental import pallas as pl
from jax.experimental.pallas import tpu as pltpu
from jax.sharding import PartitionSpec as P

HEAD = 128
TILE = 128
WIDTH = 512
F32 = jnp.float32
BF16 = jnp.bfloat16
MESH = pl.DeviceIdType.MESH


def kernel(
    sizes,
    anc_ref, slots_ref, query_ref, pairs_ref, residual_ref, weight_ref,
    hidden_ref, total_ref,
    kv, far, stage, want, want_recv, bias, q, res, w, att, near_send, near_recv,
    far_send, far_recv, own, hid, sq_send, sq_recv,
    load_sem, w_sem, out_sem, kv_recv_sem, kv_z_sem, kv_x_sem,
    x_recv_sem, want_send_sem, want_recv_sem,
    near_send_sem, near_recv_sem, far_send_sem, far_recv_sem, sq_send_sem, sq_recv_sem,
):
    dp_count, mp_count, nx, tiles, heads, kv_heads, width = sizes
    nz = dp_count // nx
    ny = mp_count // 2
    features = mp_count * width
    chunks = width // WIDTH
    me_dp, me_mp = lax.axis_index("dp"), lax.axis_index("mp")
    z, x = me_dp // nx, me_dp % nx
    y, core = me_mp // 2, me_mp % 2
    sibling = y * 2 + (1 - core)

    def dev(dp, mp):
        return {"dp": dp, "mp": mp}

    kv_head = me_mp * kv_heads // mp_count
    own_kv = pltpu.make_async_copy(
        pairs_ref.at[:, :, pl.ds(pl.multiple_of(kv_head * HEAD, HEAD), HEAD)],
        kv.at[me_dp], load_sem.at[0])
    own_kv.start()
    load_q = pltpu.make_async_copy(query_ref, q, load_sem.at[1])
    load_q.start()
    blocks = []
    for dy in list(range(1, ny)) + [0]:
        for other in (1, 0):
            block = ((y + dy) % ny) * 2 + (core if other == 0 else 1 - core)
            blocks.append(block)
    w_loads = []
    for i, block in enumerate(blocks):
        copy = pltpu.make_async_copy(
            weight_ref.at[:, pl.ds(pl.multiple_of(block * width, width), width)],
            w.at[i], w_sem.at[i])
        copy.start()
        w_loads.append(copy)
    load_res = pltpu.make_async_copy(residual_ref, res, load_sem.at[2])
    load_res.start()

    barrier = pltpu.get_barrier_semaphore()
    for dm in range(1, mp_count):
        pl.semaphore_signal(barrier, inc=1, device_id=dev(me_dp, (me_mp + dm) % mp_count), device_id_type=MESH)
    for dx in range(1, nx):
        pl.semaphore_signal(barrier, inc=1, device_id=dev(z * nx + (x + dx) % nx, me_mp), device_id_type=MESH)

    @pl.when(z > 0)
    def _():
        pl.semaphore_signal(barrier, inc=1, device_id=dev(me_dp - nx, me_mp), device_id_type=MESH)

    @pl.when(z < nz - 1)
    def _():
        pl.semaphore_signal(barrier, inc=1, device_id=dev(me_dp + nx, me_mp), device_id_type=MESH)

    ends = jnp.where(z > 0, 1, 0) + jnp.where(z < nz - 1, 1, 0)
    pl.semaphore_wait(barrier, mp_count - 1 + nx - 1 + ends)
    own_kv.wait()

    def z_copy(src, half, target, send_sem):
        return pltpu.make_async_remote_copy(
            src_ref=kv.at[src, half], dst_ref=kv.at[src, half], send_sem=send_sem,
            recv_sem=kv_recv_sem.at[half, src], device_id=dev(target, me_mp), device_id_type=MESH)

    def z_send(line, half, up):
        return z_copy(line * nx + x, half, me_dp + (nx if up else -nx), kv_z_sem.at[1 if up else 0, half, line])

    def z_arrived(line, half):
        z_copy(line * nx + x, half, me_dp, kv_z_sem.at[0, 0, 0]).wait_recv()

    def x_copy(line, half, dx, src):
        return pltpu.make_async_remote_copy(
            src_ref=stage.at[dx - 1, line, half],
            dst_ref=far.at[half, pl.ds(pl.multiple_of(src * TILE, TILE), TILE)],
            send_sem=kv_x_sem.at[dx - 1, half, line], recv_sem=x_recv_sem.at[half, src],
            device_id=dev(z * nx + (x + dx) % nx, me_mp), device_id_type=MESH)

    def want_copy(dx):
        return pltpu.make_async_remote_copy(
            src_ref=want, dst_ref=want_recv.at[dx - 1],
            send_sem=want_send_sem.at[dx - 1], recv_sem=want_recv_sem.at[dx - 1],
            device_id=dev(z * nx + (x + dx) % nx, me_mp), device_id_type=MESH)

    def select(src, half, pick):
        pick = jnp.broadcast_to(pick, (TILE, HEAD))
        best = kv[src, half, 0:TILE, :].astype(F32)
        for u in range(1, tiles):
            best = jnp.where(pick == u, kv[src, half, u * TILE:(u + 1) * TILE, :].astype(F32), best)
        return best.astype(BF16)

    def deliver(line, half):
        src = line * nx + x
        for dx in range(1, nx):
            stage[dx - 1, line, half] = select(src, half, want_recv[nx - dx - 1, src, 0:1, :])
            x_copy(line, half, dx, src).start()
        far[half, pl.ds(pl.multiple_of(src * TILE, TILE), TILE), :] = select(src, half, want[src, 0:1, :])

    for half in range(2):
        @pl.when(z < nz - 1)
        def _():
            z_send(z, half, True).start()

        @pl.when(z > 0)
        def _():
            z_send(z, half, False).start()

    def lookup(src, carry):
        picked = jnp.int32(0)
        seen = [jnp.int32(0)] * tiles
        for u in range(tiles):
            slot = src * tiles + u
            tile_id = slots_ref[slot]
            hit = jnp.int32(0)
            for t in range(tiles):
                found = jnp.int32(0)
                for j in range(anc_ref.shape[1]):
                    found = found | jnp.where(anc_ref[t, j] == tile_id, 1, 0)
                found = found * jnp.where(slot == me_dp * tiles + t, 0, 1)
                seen[t] = seen[t] | found
                hit = hit | found
            picked = picked + hit * u
        for t in range(tiles):
            column = jnp.where(jnp.full((8, TILE), seen[t]) > 0, 0.0, -jnp.inf).astype(F32)
            bias[t, :, pl.ds(pl.multiple_of(src * TILE, TILE), TILE)] = column
        want[src] = jnp.full((8, TILE), picked).astype(F32)
        return carry

    lax.fori_loop(0, dp_count, lookup, 0)
    for dx in range(1, nx):
        want_copy(dx).start()

    for d in range(1, nz):
        for half in range(2):
            @pl.when(z >= d)
            def _():
                z_arrived(z - d, half)

                @pl.when(z < nz - 1)
                def _():
                    z_send(z - d, half, True).start()

            @pl.when(z + d < nz)
            def _():
                z_arrived(z + d, half)

                @pl.when(z > 0)
                def _():
                    z_send(z + d, half, False).start()

            if d == 1 and half == 0:
                for dx in range(1, nx):
                    want_copy(dx).wait_recv()
                for part in range(2):
                    deliver(z, part)

            @pl.when(z >= d)
            def _():
                deliver(z - d, half)

            @pl.when(z + d < nz)
            def _():
                deliver(z + d, half)

    if nz == 1:
        for dx in range(1, nx):
            want_copy(dx).wait_recv()
        for part in range(2):
            deliver(z, part)

    load_q.wait()
    for dx in range(1, nx):
        for line in range(nz):
            for half in range(2):
                x_copy(line, half, dx, line * nx + (x + dx) % nx).wait_recv()

    pair = 2 if heads % 2 == 0 else 1
    exponent = HEAD ** (-0.5) * math.log2(math.e)
    causal = (
        lax.broadcasted_iota(jnp.int32, (TILE, TILE), 0)
        >= lax.broadcasted_iota(jnp.int32, (TILE, TILE), 1)
    )
    causal = jnp.concatenate([causal] * pair, axis=0)

    def attention(t):
        rows = slice(t * TILE, (t + 1) * TILE)

        def step(hp, carry):
            columns = pl.ds(pl.multiple_of(hp * (pair * HEAD), pair * HEAD), pair * HEAD)
            both = q[rows, columns]
            stacked = jnp.concatenate([both[:, i * HEAD:(i + 1) * HEAD] for i in range(pair)], axis=0)
            near = lax.dot_general(
                stacked, kv[me_dp, 0, rows, :], (((1,), (1,)), ((), ())), preferred_element_type=F32)
            scores = lax.dot_general(stacked, far[0], (((1,), (1,)), ((), ())), preferred_element_type=F32)
            near = jnp.where(causal, near, -jnp.inf)
            scores = scores + bias[t, 0:1, :]
            peak = jnp.maximum(jnp.max(scores, axis=1, keepdims=True), jnp.max(near, axis=1, keepdims=True))
            near = jnp.exp2((near - peak) * exponent)
            weights = jnp.exp2((scores - peak) * exponent)
            totals = jnp.sum(weights, axis=1, keepdims=True) + jnp.sum(near, axis=1, keepdims=True)
            mixed = jnp.dot(weights.astype(BF16), far[1], preferred_element_type=F32)
            mixed = mixed + jnp.dot(near.astype(BF16), kv[me_dp, 1, rows, :], preferred_element_type=F32)
            mixed = mixed / totals
            mixed = mixed.astype(BF16)
            att[rows, columns] = jnp.concatenate([mixed[i * TILE:(i + 1) * TILE] for i in range(pair)], axis=1)
            return carry

        lax.fori_loop(0, heads // pair, step, 0)

    def project(t, i, j):
        return jnp.dot(att[t * TILE:(t + 1) * TILE, :], w[i, :, j * WIDTH:(j + 1) * WIDTH], preferred_element_type=F32)

    def near_copy(t, dy, j):
        return pltpu.make_async_remote_copy(
            src_ref=near_send.at[dy, t, j], dst_ref=near_recv.at[dy, t, j],
            send_sem=near_send_sem.at[dy, t, j], recv_sem=near_recv_sem.at[dy, t, j],
            device_id=dev(me_dp, sibling), device_id_type=MESH)

    def far_copy(t, dy, j):
        return pltpu.make_async_remote_copy(
            src_ref=far_send.at[dy - 1, t, j], dst_ref=far_recv.at[dy - 1, t, j],
            send_sem=far_send_sem.at[dy - 1, t, j], recv_sem=far_recv_sem.at[dy - 1, t, j],
            device_id=dev(me_dp, ((y + dy) % ny) * 2 + core), device_id_type=MESH)

    def sq_copy(t, dm):
        return pltpu.make_async_remote_copy(
            src_ref=sq_send.at[t], dst_ref=sq_recv.at[t, dm - 1],
            send_sem=sq_send_sem.at[t, dm - 1], recv_sem=sq_recv_sem.at[t, dm - 1],
            device_id=dev(me_dp, (me_mp + dm) % mp_count), device_id_type=MESH)

    def give(t, dy, j):
        i = 2 * ((dy - 1) % ny)
        near_send[dy, t, j] = project(t, i, j).astype(BF16)
        near_copy(t, dy, j).start()

    def take(t, dy, j):
        i = 2 * ((dy - 1) % ny) + 1
        part = project(t, i, j)
        if dy == 0:
            own[t, j] = part
            return
        near_copy(t, dy, j).wait_recv()
        far_send[dy - 1, t, j] = (part + near_recv[dy, t, j].astype(F32)).astype(BF16)
        far_copy(t, dy, j).start()

    def run(t, dys):
        work = [(dy, j) for dy in dys for j in range(chunks)]
        for n in range(len(work) + 1):
            if n < len(work):
                give(t, *work[n])
            if n > 0:
                take(t, *work[n - 1])

    far_dys = list(range(1, ny))
    for t in range(tiles):
        attention(t)
        if t == 0:
            for copy in w_loads:
                copy.wait()
        run(t, far_dys)
    for t in range(tiles):
        run(t, [0])

    load_res.wait()

    def gather(t):
        rows = slice(t * TILE, (t + 1) * TILE)
        square = jnp.zeros((TILE, HEAD), F32)
        for j in range(chunks):
            near_copy(t, 0, j).wait_recv()
            for dy in far_dys:
                far_copy(t, dy, j).wait_recv()
            total = own[t, j] + near_recv[0, t, j].astype(F32)
            for dy in far_dys:
                total = total + far_recv[dy - 1, t, j].astype(F32)
            columns = slice(j * WIDTH, (j + 1) * WIDTH)
            out = (res[rows, columns].astype(F32) + total).astype(BF16)
            hid[rows, columns] = out
            out = out.astype(F32)
            out = out * out
            for k in range(WIDTH // HEAD):
                square = square + out[:, k * HEAD:(k + 1) * HEAD]
        line = jnp.broadcast_to(jnp.sum(square, axis=1, keepdims=True), (TILE, TILE))
        sq_send[t] = jnp.transpose(line)[0:8, :]
        for dm in range(1, mp_count):
            sq_copy(t, dm).start()
        pltpu.make_async_copy(hid.at[pl.ds(t * TILE, TILE)], hidden_ref.at[pl.ds(t * TILE, TILE)], out_sem.at[t]).start()

    def finish(t):
        total = sq_send[t]
        for dm in range(1, mp_count):
            sq_copy(t, dm).wait_recv()
            total = total + sq_recv[t, dm - 1]
        total_ref[t] = total

    for t in range(tiles):
        gather(t)
        if t > 0:
            finish(t - 1)

    for line in range(nz):
        for half in range(2):
            @pl.when((z < nz - 1) & (z >= line))
            def _():
                z_send(line, half, True).wait_send()

            @pl.when((z > 0) & (z <= line))
            def _():
                z_send(line, half, False).wait_send()

            for dx in range(1, nx):
                x_copy(line, half, dx, me_dp).wait_send()
    for dx in range(1, nx):
        want_copy(dx).wait_send()
    for t in range(tiles):
        for j in range(chunks):
            for dy in range(ny):
                near_copy(t, dy, j).wait_send()
            for dy in far_dys:
                far_copy(t, dy, j).wait_send()
    finish(tiles - 1)
    for t in range(tiles):
        for dm in range(1, mp_count):
            sq_copy(t, dm).wait_send()
        pltpu.make_async_copy(hid.at[pl.ds(t * TILE, TILE)], hidden_ref.at[pl.ds(t * TILE, TILE)], out_sem.at[t]).wait()


def norm_kernel(features, hidden_ref, total_ref, gain_ref, out_ref, normed_ref, hid, nrm, in_sem, out_sem):
    tiles = total_ref.shape[0]

    def part(t):
        return pl.ds(t * TILE, TILE)

    for t in range(tiles):
        pltpu.make_async_copy(hidden_ref.at[part(t)], hid.at[part(t)], in_sem.at[t]).start()
    for t in range(tiles):
        rows = slice(t * TILE, (t + 1) * TILE)
        line = lax.rsqrt(total_ref[t, 0:1, :] / features + 1e-05)
        scale = jnp.transpose(jnp.broadcast_to(line, (TILE, TILE)))
        pltpu.make_async_copy(hidden_ref.at[part(t)], hid.at[part(t)], in_sem.at[t]).wait()
        pltpu.make_async_copy(hid.at[part(t)], out_ref.at[part(t)], out_sem.at[0, t]).start()
        for k in range(gain_ref.shape[1] // HEAD):
            columns = slice(k * HEAD, (k + 1) * HEAD)
            nrm[rows, columns] = (hid[rows, columns].astype(F32) * scale * gain_ref[0:1, columns]).astype(BF16)
        pltpu.make_async_copy(nrm.at[part(t)], normed_ref.at[part(t)], out_sem.at[1, t]).start()
    for t in range(tiles):
        pltpu.make_async_copy(hid.at[part(t)], out_ref.at[part(t)], out_sem.at[0, t]).wait()
        pltpu.make_async_copy(nrm.at[part(t)], normed_ref.at[part(t)], out_sem.at[1, t]).wait()


def solution(mesh):
    dp_count, mp_count = mesh.shape["dp"], mesh.shape["mp"]
    nx = 2 ** (int(math.log2(dp_count)) // 2)
    if dp_count % nx:
        nx = 1
    ny = mp_count // 2

    def body(query, keys_values, ancestors, tile_of_slot, residual, norm_gain, out_weight):
        tokens, inner = query.shape
        tiles, heads = tokens // TILE, inner // HEAD
        width = residual.shape[1]
        kv_heads = keys_values.shape[2] // HEAD
        chunks = width // WIDTH
        sizes = (dp_count, mp_count, nx, tiles, heads, kv_heads, width)
        dma = pltpu.SemaphoreType.DMA
        anywhere = pl.BlockSpec(memory_space=pl.ANY)
        smem = pl.BlockSpec(memory_space=pltpu.SMEM)
        span = dp_count * TILE
        fx = max(nx - 1, 1)
        vmem = pl.BlockSpec(memory_space=pltpu.VMEM)
        nz = dp_count // nx
        fy = max(ny - 1, 1)
        hidden, total = pl.pallas_call(
            functools.partial(kernel, sizes),
            out_shape=(jax.ShapeDtypeStruct(residual.shape, BF16), jax.ShapeDtypeStruct((tiles, 8, TILE), F32)),
            in_specs=[smem, smem] + [anywhere] * 4,
            out_specs=(anywhere, vmem),
            scratch_shapes=[
                pltpu.VMEM((dp_count, 2, tokens, HEAD), BF16),
                pltpu.VMEM((2, span, HEAD), BF16),
                pltpu.VMEM((fx, nz, 2, TILE, HEAD), BF16),
                pltpu.VMEM((dp_count, 8, TILE), F32),
                pltpu.VMEM((fx, dp_count, 8, TILE), F32),
                pltpu.VMEM((tiles, 8, span), F32),
                pltpu.VMEM((tokens, inner), BF16),
                pltpu.VMEM((tokens, width), BF16),
                pltpu.VMEM((mp_count, inner, width), BF16),
                pltpu.VMEM((tokens, inner), BF16),
                pltpu.VMEM((ny, tiles, chunks, TILE, WIDTH), BF16),
                pltpu.VMEM((ny, tiles, chunks, TILE, WIDTH), BF16),
                pltpu.VMEM((fy, tiles, chunks, TILE, WIDTH), BF16),
                pltpu.VMEM((fy, tiles, chunks, TILE, WIDTH), BF16),
                pltpu.VMEM((tiles, chunks, TILE, WIDTH), F32),
                pltpu.VMEM((tokens, width), BF16),
                pltpu.VMEM((tiles, 8, TILE), F32),
                pltpu.VMEM((tiles, mp_count - 1, 8, TILE), F32),
                dma((4,)), dma((mp_count,)), dma((tiles,)),
                dma((2, dp_count)), dma((2, 2, nz)), dma((fx, 2, nz)),
                dma((2, dp_count)), dma((fx,)), dma((fx,)),
                dma((ny, tiles, chunks)), dma((ny, tiles, chunks)),
                dma((fy, tiles, chunks)), dma((fy, tiles, chunks)),
                dma((tiles, mp_count - 1)), dma((tiles, mp_count - 1)),
            ],
            compiler_params=pltpu.CompilerParams(
                collective_id=0, has_side_effects=True, vmem_limit_bytes=56 * 1024 * 1024),
        )(ancestors, tile_of_slot, query, keys_values, residual, out_weight)
        return pl.pallas_call(
            functools.partial(norm_kernel, mp_count * width),
            out_shape=(jax.ShapeDtypeStruct(residual.shape, BF16),) * 2,
            in_specs=[anywhere, vmem, vmem],
            out_specs=(anywhere, anywhere),
            scratch_shapes=[
                pltpu.VMEM((tokens, width), BF16),
                pltpu.VMEM((tokens, width), BF16),
                dma((tiles,)), dma((2, tiles)),
            ],
            compiler_params=pltpu.CompilerParams(vmem_limit_bytes=56 * 1024 * 1024),
        )(hidden, total, norm_gain.reshape(1, width))

    return jax.shard_map(
        body,
        mesh=mesh,
        in_specs=(
            P("dp", "mp"),
            P(None, "dp", None),
            P("dp", None),
            P(),
            P("dp", "mp"),
            P("mp"),
            P("mp", None),
        ),
        out_specs=(P("dp", "mp"), P("dp", "mp")),
        check_vma=False,
    )
```

time: 62.4 us -> 58 us (0.929)
  local copies, waits for them, and re-layouts: 4.61 us -> 0 us
    unnamed x2 -> x0, local copies, waits for them, and re-layouts: 4.61 us -> none
    pallas_call x0 -> x1, Pallas kernels: none -> 3.16 us  [body(): pl.pallas_call(functools.partial(norm_kernel, mp_count * width), out_shap...]
    pallas_call x1, Pallas kernels: 56.9 us -> 54 us  [body(): pl.pallas_call(functools.partial(kernel, sizes), out_shape=(jax.ShapeDtyp...]
where the time goes in v2:
time: 58 us; the launch traced here: 57.8 us
  Pallas kernels  57.1 us (98%)
  between operations  0.64 us (1%)
    pallas_call x1, Pallas kernels, body(): pl.pallas_call(functools.partial(kernel, sizes), out_shape=(jax.ShapeDtyp...  54 us
    pallas_call x1, Pallas kernels, body(): pl.pallas_call(functools.partial(norm_kernel, mp_count * width), out_shap...  3.16 us

profile of v2, /device:TPU:0, one launch (start us, length us, event | category | flops | bytes accessed | tf_op | source)
XLA Modules:
  0.0 57.8 jit_solution(14221932416894989714)
XLA Ops:
  0.6 54.0 %shard_map.86 = (bf16[256,2048]{1,0:T(8,128)(2,1)}, f32[2,8,128]{2,1,0:T(8,128)}) custom-call(s32[2,12]{1,0:T(2,128)} %anc_ref.1, s32[16]{0:T(128)} %slots_ref.1, bf16[256,1024]{1,0:T(8,128)(2,1)} %query_ref.1, bf16[2,256,512]{2,1,0:T(8,128)(2,1)} %pairs_ref.1, bf16[256,2048]{1,0:T(8,128)(2,1)} %residual_ref.1, bf16[1024,8192]{1,0:T(8,128)(2,1)} %weight_ref.1), custom_call_target="tpu_custom_call" | custom-call | tf_op jit(solution)/shard_map/pallas_call | solution.py:394
  54.6 3.2 %shard_map.87 = (bf16[256,2048]{1,0:T(8,128)(2,1)}, bf16[256,2048]{1,0:T(8,128)(2,1)}) custom-call(bf16[256,2048]{1,0:T(8,128)(2,1)} %get-tuple-element.4.hidden_ref, f32[2,8,128]{2,1,0:T(8,128)} %get-tuple-element.5.total_ref, f32[1,2048]{1,0:T(1,128)} %bitcast.1), custom_call_target="tpu_custom_call" | custom-call | tf_op jit(solution)/shard_map/pallas_call | solution.py:428

commit v3 on v2

--- a/solution.py
+++ b/solution.py
@@ -169,19 +169,25 @@
                 def _():
                     z_send(z + d, half, False).start()
 
-            if d == 1 and half == 0:
+            if half == 1 and d == 1:
                 for dx in range(1, nx):
                     want_copy(dx).wait_recv()
                 for part in range(2):
                     deliver(z, part)
 
-            @pl.when(z >= d)
-            def _():
-                deliver(z - d, half)
-
-            @pl.when(z + d < nz)
-            def _():
-                deliver(z + d, half)
+            ready = [half] if d == nz - 1 else [0, 1] if half == 1 else []
+            if d == 1 and half == 0:
+                ready = []
+            elif d == 1 and half == 1:
+                ready = [0, 1]
+            for part in ready:
+                @pl.when(z >= d)
+                def _():
+                    deliver(z - d, part)
+
+                @pl.when(z + d < nz)
+                def _():
+                    deliver(z + d, part)
 
     if nz == 1:
         for dx in range(1, nx):
@@ -226,7 +232,7 @@
             att[rows, columns] = jnp.concatenate([mixed[i * TILE:(i + 1) * TILE] for i in range(pair)], axis=1)
             return carry
 
-        lax.fori_loop(0, heads // pair, step, 0)
+        lax.fori_loop(0, heads // pair, step, 0, unroll=True)
 
     def project(t, i, j):
         return jnp.dot(att[t * TILE:(t + 1) * TILE, :], w[i, :, j * WIDTH:(j + 1) * WIDTH], preferred_element_type=F32)

time: 58 us -> 57.2 us (0.986)
  Pallas kernels: 57.1 us -> 56.2 us
    pallas_call x1, Pallas kernels: 54 us -> 53.1 us  [body(): pl.pallas_call(functools.partial(kernel, sizes), out_shape=(jax.ShapeDtyp...]
where the time goes in v3:
time: 57.2 us; the launch traced here: 56.9 us
  Pallas kernels  56.2 us (98%)
  between operations  0.64 us (1%)
    pallas_call x1, Pallas kernels, body(): pl.pallas_call(functools.partial(kernel, sizes), out_shape=(jax.ShapeDtyp...  53.1 us
    pallas_call x1, Pallas kernels, body(): pl.pallas_call(functools.partial(norm_kernel, mp_count * width), out_shap...  3.16 us

profile of v3, /device:TPU:0, one launch (start us, length us, event | category | flops | bytes accessed | tf_op | source)
XLA Modules:
  0.0 56.9 jit_solution(15743163770263724814)
XLA Ops:
  0.6 53.1 %shard_map.86 = (bf16[256,2048]{1,0:T(8,128)(2,1)}, f32[2,8,128]{2,1,0:T(8,128)}) custom-call(s32[2,12]{1,0:T(2,128)} %anc_ref.1, s32[16]{0:T(128)} %slots_ref.1, bf16[256,1024]{1,0:T(8,128)(2,1)} %query_ref.1, bf16[2,256,512]{2,1,0:T(8,128)(2,1)} %pairs_ref.1, bf16[256,2048]{1,0:T(8,128)(2,1)} %residual_ref.1, bf16[1024,8192]{1,0:T(8,128)(2,1)} %weight_ref.1), custom_call_target="tpu_custom_call" | custom-call | tf_op jit(solution)/shard_map/pallas_call | solution.py:400
  53.7 3.2 %shard_map.87 = (bf16[256,2048]{1,0:T(8,128)(2,1)}, bf16[256,2048]{1,0:T(8,128)(2,1)}) custom-call(bf16[256,2048]{1,0:T(8,128)(2,1)} %get-tuple-element.4.hidden_ref, f32[2,8,128]{2,1,0:T(8,128)} %get-tuple-element.5.total_ref, f32[1,2048]{1,0:T(1,128)} %bitcast.1), custom_call_target="tpu_custom_call" | custom-call | tf_op jit(solution)/shard_map/pallas_call | solution.py:434
